TPU v7x, 32 devices: a whole 2x2x4 slice. The times are simulated.
32 devices in a mesh: grp: 4 (over x, core), tile: 8 (over z, y).
Axes of the slice: x: 2, y: 2, z: 4, core: 2. Of those that a mesh axis runs over, the one named last changes fastest.
Arguments:
- height_model: float32 [4608, 1024], P('grp', 'tile'), as said below
- scenario_trigger_indicator: int32 [4, 256, 512], P('grp', 'tile'), may hold values 0 or 1
- initial_snow_thickness_cm: int32 [4, 256, 512], P('grp', 'tile'), may hold values from 20 to 300
- frame_leading_northing_index: int32 [4], P('grp'), may hold values from 3 to 4349
- frame_leading_easting_index: int32 [4], P('grp'), may hold values from 3 to 509
Outputs:
- ground_geometry: float32 [4, 4608, 1024], P(None, 'grp', 'tile')
- flow: float32 [4, 3, 256, 512], P('grp', None, 'tile')
Inputs may be any that keep to these rules, and one draw needn't show every extreme that they name: `frame_leading_northing_index`: each window, widened by 3 cells on every side, lies inside the DEM rows. `frame_leading_easting_index`: each window, widened by 3 cells on every side, lies inside the DEM columns. `height_model`: elevation in metres, near zero at the DEM's rim within a few metres.
All inputs are finite; a program needn't handle non-finite values. No bound on the sum of `scenario_trigger_indicator` on one device may be relied on, other than what follows from the above.
Results may differ from a plain program's by a relative error of at most 0.0003.
Values sent between devices are 32-bit elements; how exact they have to be, the bound alone decides.
A program may use at most 64 MiB of HBM per device.

v0:
```python
import jax
import jax.numpy as jnp
from jax import lax
from jax.sharding import PartitionSpec as P

KERNEL_SPAN = 3
STEPS = 4
cell_size = 2.0
gravity = 9.81
time_step = 0.1
friction = 0.2
turbulence = 500.0
depth_floor = 0.1
speed_floor = 0.5
binomial = (0.0625, 0.25, 0.375, 0.25, 0.0625)


def padded(shard, sides, width):
    for axis, dim in sides:
        size, length = (lax.axis_size(axis), shard.shape[dim])
        up = [(i, (i + 1) % size) for i in range(size - 1)]
        down = [(j, i) for i, j in up]
        last = lax.slice_in_dim(shard, length - width, length, axis=dim)
        leading = lax.slice_in_dim(shard, 0, width, axis=dim)
        before = lax.ppermute(last, axis, up)
        after = lax.ppermute(leading, axis, down)
        shard = jnp.concatenate([before, shard, after], axis=dim)
    return shard


def derive_gradient_fields(framed_elevation_grid):
    inner_rows = framed_elevation_grid.shape[0] - 2 * KERNEL_SPAN
    inner_cols = framed_elevation_grid.shape[1] - 2 * KERNEL_SPAN
    across = binomial[0] * framed_elevation_grid[0 : inner_rows + 2, :]
    for offset in range(1, 5):
        across = (
            across + binomial[offset] * framed_elevation_grid[offset : offset + inner_rows + 2, :]
        )
    smooth = binomial[0] * across[:, 0 : inner_cols + 2]
    for offset in range(1, 5):
        smooth = smooth + binomial[offset] * across[:, offset : offset + inner_cols + 2]
    centre = smooth[1:-1, 1:-1]
    upper_cell = smooth[2:, 1:-1]
    lower_cell = smooth[:-2, 1:-1]
    right_cell = smooth[1:-1, 2:]
    left_cell = smooth[1:-1, :-2]
    grad_rows = (upper_cell - lower_cell) / (2.0 * cell_size)
    grad_cols = (right_cell - left_cell) / (2.0 * cell_size)
    curvature = (upper_cell + lower_cell + right_cell + left_cell - 4.0 * centre) / (
        cell_size * cell_size
    )
    upright = 1.0 / jnp.sqrt(1.0 + grad_rows * grad_rows + grad_cols * grad_cols)
    return jnp.stack([-grad_rows * upright, -grad_cols * upright, upright, curvature])


def advance(framed_elevation_grid, patch):
    depth_now = framed_elevation_grid[0]
    momentum_a = framed_elevation_grid[1]
    momentum_b = framed_elevation_grid[2]
    safe_depth = jnp.maximum(depth_now, depth_floor)
    velocity_a = momentum_a / safe_depth
    velocity_b = momentum_b / safe_depth
    wave_speed = jnp.sqrt(gravity * (jnp.maximum(depth_now, 0.0) + depth_floor))
    pressure = 0.5 * gravity * depth_now * depth_now
    flux_rows = jnp.stack([momentum_a, momentum_a * velocity_a + pressure, momentum_b * velocity_a])
    flux_cols = jnp.stack([momentum_b, momentum_a * velocity_b, momentum_b * velocity_b + pressure])
    reach_rows = jnp.abs(velocity_a) + wave_speed
    reach_cols = jnp.abs(velocity_b) + wave_speed
    bound_rows = jnp.maximum(reach_rows[:-1, 1:-1], reach_rows[1:, 1:-1])
    face_rows = 0.5 * (flux_rows[:, :-1, 1:-1] + flux_rows[:, 1:, 1:-1]) - 0.5 * bound_rows * (
        framed_elevation_grid[:, 1:, 1:-1] - framed_elevation_grid[:, :-1, 1:-1]
    )
    bound_cols = jnp.maximum(reach_cols[1:-1, :-1], reach_cols[1:-1, 1:])
    face_cols = 0.5 * (flux_cols[:, 1:-1, :-1] + flux_cols[:, 1:-1, 1:]) - 0.5 * bound_cols * (
        framed_elevation_grid[:, 1:-1, 1:] - framed_elevation_grid[:, 1:-1, :-1]
    )
    interior = framed_elevation_grid[:, 1:-1, 1:-1]
    updated = interior - time_step / cell_size * (
        face_rows[:, 1:] - face_rows[:, :-1] + face_cols[:, :, 1:] - face_cols[:, :, :-1]
    )
    new_depth = updated[0]
    drive_a = updated[1] + time_step * gravity * interior[0] * patch[0]
    drive_b = updated[2] + time_step * gravity * interior[0] * patch[1]
    floor_depth = jnp.maximum(new_depth, depth_floor)
    rate_a = drive_a / floor_depth
    rate_b = drive_b / floor_depth
    square = rate_a * rate_a + rate_b * rate_b
    speed_norm = jnp.sqrt(square + speed_floor * speed_floor)
    normal_load = jnp.maximum(gravity * patch[2] + patch[3] * square, 0.0)
    drag_factor = time_step * (
        friction * normal_load / speed_norm + gravity * speed_norm / (turbulence * floor_depth)
    )
    return jnp.stack([new_depth, drive_a / (1.0 + drag_factor), drive_b / (1.0 + drag_factor)])


def shards(
    height_model,
    scenario_trigger_indicator,
    initial_snow_thickness_cm,
    frame_leading_northing_index,
    frame_leading_easting_index,
):
    tile_count = lax.axis_size("tile")
    piece_rows = scenario_trigger_indicator.shape[1]
    window_width = scenario_trigger_indicator.shape[2]
    window_height = piece_rows * tile_count
    block_lateral_number = height_model.shape[1]
    framed_elevation_grid = padded(height_model, (("grp", 0), ("tile", 1)), KERNEL_SPAN)
    ground_geometry = derive_gradient_fields(framed_elevation_grid)
    first_row = frame_leading_northing_index[0]
    first_col = frame_leading_easting_index[0]
    column_strip = lax.all_gather(ground_geometry, "grp", axis=1, tiled=True)
    row_band = lax.dynamic_slice_in_dim(column_strip, first_row, window_height, 1)
    blocks = row_band.reshape(4, tile_count, piece_rows, block_lateral_number)
    rows_wide = lax.all_to_all(blocks, "tile", split_axis=1, concat_axis=3, tiled=True)
    rows_wide = rows_wide.reshape(4, piece_rows, tile_count * block_lateral_number)
    under_window = lax.dynamic_slice_in_dim(rows_wide, first_col, window_width, 2)
    release_depth = (
        scenario_trigger_indicator[0].astype(jnp.float32)
        * initial_snow_thickness_cm[0].astype(jnp.float32)
        * 0.01
    )
    empty_field = jnp.zeros_like(release_depth)
    flow_state = jnp.stack([release_depth, empty_field, empty_field])
    for turn_index in range(STEPS):
        extended = padded(flow_state, (("tile", 1),), 1)
        flow_state = advance(jnp.pad(extended, ((0, 0), (0, 0), (1, 1))), under_window)
    return (ground_geometry, flow_state[None])


def solution(mesh):
    return jax.shard_map(
        shards,
        mesh=mesh,
        in_specs=(
            P("grp", "tile"),
            P("grp", "tile", None),
            P("grp", "tile", None),
            P("grp"),
            P("grp"),
        ),
        out_specs=(P(None, "grp", "tile"), P("grp", None, "tile", None)),
        check_vma=False,
    )
```

profile of v0, /device:TPU:16, one launch (start us, length us, event | category | flops | bytes accessed | tf_op | source)
XLA Modules:
  0.0 159.4 jit_solution(9979088048718649279)
XLA Ops:
  7.2 0.7 fusion.58
  7.9 1.7 %collective-permute-start = (f32[3,128]{1,0:T(4,128)S(1)}, f32[3,128]{1,0:T(4,128)S(1)}, u32[]{:S(2)}, u32[]{:S(2)}) collective-permute-start(f32[3,128]{1,0:T(4,128)S(1)} %get-tuple-element.21), channel_id=1, source_target_pairs={{0,8},{8,16},{16,24},{1,9},{9,17},{17,25},{2,10},{10,18},{18,26},{... | collective-permute-start | bytes 4616 | tf_op jit(solution)/shard_map/ppermute | solution.py:25
  9.7 1.3 collective-permute-start.1
  11.0 3.0 %collective-permute-done.1 = f32[3,128]{1,0:T(4,128)S(1)} collective-permute-done((f32[3,128]{1,0:T(4,128)S(1)}, f32[3,128]{1,0:T(4,128)S(1)}, u32[]{:S(2)}, u32[]{:S(2)}) %collective-permute-start.1) | collective-permute-done | bytes 1568 | tf_op jit(solution)/shard_map/ppermute | solution.py:26
  14.0 2.3 %concatenate.42 = f32[1158,128]{1,0:T(8,128)S(1)} concatenate(f32[3,128]{1,0:T(4,128)S(1)} %collective-permute-done, f32[1152,128]{1,0:T(8,128)} %param.5, f32[3,128]{1,0:T(4,128)S(1)} %collective-permute-done.1), dimensions={0} | concatenate | bytes 1185792 | tf_op jit(solution)/shard_map/concatenate | solution.py:27
  16.3 0.2 fusion.57
  16.5 0.2 copy.9
  16.7 3.3 %collective-permute-start.3 = (f32[1158,3]{0,1:T(4,128)S(1)}, f32[1158,3]{0,1:T(4,128)S(1)}, u32[]{:S(2)}, u32[]{:S(2)}) collective-permute-start(f32[1158,3]{0,1:T(4,128)S(1)} %copy.9), channel_id=1, source_target_pairs={{1,0},{2,1},{3,2},{4,3},{5,4},{6,5},{7,6},{9,8},{10,9},{11,10},{12... | collective-permute-start | bytes 41696 | tf_op jit(solution)/shard_map/ppermute | solution.py:26
  20.0 0.2 copy.8
  20.2 2.5 %collective-permute-start.2 = (f32[1158,3]{0,1:T(4,128)S(1)}, f32[1158,3]{0,1:T(4,128)S(1)}, u32[]{:S(2)}, u32[]{:S(2)}) collective-permute-start(f32[1158,3]{0,1:T(4,128)S(1)} %copy.8), channel_id=1, source_target_pairs={{0,1},{1,2},{2,3},{3,4},{4,5},{5,6},{6,7},{8,9},{9,10},{10,11},{11... | collective-permute-start | bytes 41696 | tf_op jit(solution)/shard_map/ppermute | solution.py:25
  22.8 0.2 copy.11
  23.1 3.8 %collective-permute-done.2 = f32[1158,3]{0,1:T(4,128)S(1)} collective-permute-done((f32[1158,3]{0,1:T(4,128)S(1)}, f32[1158,3]{0,1:T(4,128)S(1)}, u32[]{:S(2)}, u32[]{:S(2)}) %collective-permute-start.2) | collective-permute-done | bytes 13928 | tf_op jit(solution)/shard_map/ppermute | solution.py:25
  26.8 0.2 copy.10
  27.1 0.5 pad_maximum_fusion.1
  27.6 0.7 fusion.4
  28.3 1.3 fusion
  29.6 0.7 multiply_bitcast_fusion.1
  30.3 1.6 pad_maximum_fusion
  31.9 0.8 copy-done
  32.8 1.9 %collective-permute-start.5 = (f32[3,1,512]{2,1,0:T(1,128)S(1)}, f32[3,1,512]{2,1,0:T(1,128)S(1)}, u32[]{:S(2)}, u32[]{:S(2)}) collective-permute-start(f32[3,1,512]{2,1,0:T(1,128)S(1)} %get-tuple-element.65), channel_id=1, source_target_pairs={{1,0},{2,1},{3,2},{4,3},{5,4},{6,5},{7,6},{9,8},{10,9},{11,10},{12... | collective-permute-start | bytes 18440 | tf_op jit(solution)/shard_map/ppermute | solution.py:26
  34.7 3.9 %collective-permute-start.4 = (f32[3,1,512]{2,1,0:T(1,128)S(1)}, f32[3,1,512]{2,1,0:T(1,128)S(1)}, u32[]{:S(2)}, u32[]{:S(2)}) collective-permute-start(f32[3,1,512]{2,1,0:T(1,128)S(1)} %get-tuple-element.64), channel_id=1, source_target_pairs={{0,1},{1,2},{2,3},{3,4},{4,5},{5,6},{6,7},{8,9},{9,10},{10,11},{11... | collective-permute-start | bytes 18440 | tf_op jit(solution)/shard_map/ppermute | solution.py:25
  40.0 1.1 collective-permute-done.4
  41.6 55.6 %all-gather.2.cloned.1.call-done = f32[4,4608,128]{2,1,0:T(8,128)} async-done(((f32[4,1152,128]{2,1,0:T(8,128)}), f32[4,4608,128]{2,1,0:T(8,128)}) %all-gather.2.cloned.1.call-update) | async-done | bytes 9437200 | tf_op jit(solution)/shard_map/all_gather | solution.py:112
  97.2 1.1 constant_dynamic-slice_fusion
  98.3 0.8 copy.12
  99.1 6.0 %all-to-all-start = ((f32[4,8,32,128]{3,2,0,1:T(8,128)}), f32[4,8,32,128]{3,2,0,1:T(8,128)S(1)}, u32[]{:S(2)}, u32[]{:S(2)}) async-start(f32[4,8,32,128]{3,2,0,1:T(8,128)} %copy.12), calls=%async_computation | async-start | bytes 1048576 | tf_op jit(solution)/shard_map/all_to_all | solution.py:115
  105.3 0.2 fusion.31
  105.5 0.2 fusion.28
  105.8 11.5 %all-to-all-done = f32[4,8,32,128]{3,2,0,1:T(8,128)S(1)} async-done(((f32[4,8,32,128]{3,2,0,1:T(8,128)}), f32[4,8,32,128]{3,2,0,1:T(8,128)S(1)}, u32[]{:S(2)}, u32[]{:S(2)}) %all-to-all-start) | async-done | bytes 524320 | tf_op jit(solution)/shard_map/all_to_all | solution.py:115
  117.3 0.3 copy.13
  117.9 2.9 %collective-permute-start.7 = (f32[3,1,512]{2,1,0:T(1,128)S(1)}, f32[3,1,512]{2,1,0:T(1,128)S(1)}, u32[]{:S(2)}, u32[]{:S(2)}) collective-permute-start(f32[3,1,512]{2,1,0:T(1,128)S(1)} %get-tuple-element.62), channel_id=1, source_target_pairs={{1,0},{2,1},{3,2},{4,3},{5,4},{6,5},{7,6},{9,8},{10,9},{11,10},{12... | collective-permute-start | bytes 18440 | tf_op jit(solution)/shard_map/ppermute | solution.py:26
  120.8 3.0 %collective-permute-start.6 = (f32[3,1,512]{2,1,0:T(1,128)S(1)}, f32[3,1,512]{2,1,0:T(1,128)S(1)}, u32[]{:S(2)}, u32[]{:S(2)}) collective-permute-start(f32[3,1,512]{2,1,0:T(1,128)S(1)} %get-tuple-element.61), channel_id=1, source_target_pairs={{0,1},{1,2},{2,3},{3,4},{4,5},{5,6},{6,7},{8,9},{9,10},{10,11},{11... | collective-permute-start | bytes 18440 | tf_op jit(solution)/shard_map/ppermute | solution.py:25
  123.8 3.4 %collective-permute-done.6 = f32[3,1,512]{2,1,0:T(1,128)S(1)} collective-permute-done((f32[3,1,512]{2,1,0:T(1,128)S(1)}, f32[3,1,512]{2,1,0:T(1,128)S(1)}, u32[]{:S(2)}, u32[]{:S(2)}) %collective-permute-start.6) | collective-permute-done | bytes 6176 | tf_op jit(solution)/shard_map/ppermute | solution.py:25
  127.2 0.2 select_maximum_fusion.8
  127.8 0.2 fusion.23
  128.0 0.2 fusion.26
  128.6 3.7 %collective-permute-start.9 = (f32[3,1,512]{2,1,0:T(1,128)S(1)}, f32[3,1,512]{2,1,0:T(1,128)S(1)}, u32[]{:S(2)}, u32[]{:S(2)}) collective-permute-start(f32[3,1,512]{2,1,0:T(1,128)S(1)} %get-tuple-element.59), channel_id=1, source_target_pairs={{1,0},{2,1},{3,2},{4,3},{5,4},{6,5},{7,6},{9,8},{10,9},{11,10},{12... | collective-permute-start | bytes 18440 | tf_op jit(solution)/shard_map/ppermute | solution.py:26
  132.3 2.1 %collective-permute-start.8 = (f32[3,1,512]{2,1,0:T(1,128)S(1)}, f32[3,1,512]{2,1,0:T(1,128)S(1)}, u32[]{:S(2)}, u32[]{:S(2)}) collective-permute-start(f32[3,1,512]{2,1,0:T(1,128)S(1)} %get-tuple-element.58), channel_id=1, source_target_pairs={{0,1},{1,2},{2,3},{3,4},{4,5},{5,6},{6,7},{8,9},{9,10},{10,11},{11... | collective-permute-start | bytes 18440 | tf_op jit(solution)/shard_map/ppermute | solution.py:25
  134.5 4.3 %collective-permute-done.8 = f32[3,1,512]{2,1,0:T(1,128)S(1)} collective-permute-done((f32[3,1,512]{2,1,0:T(1,128)S(1)}, f32[3,1,512]{2,1,0:T(1,128)S(1)}, u32[]{:S(2)}, u32[]{:S(2)}) %collective-permute-start.8) | collective-permute-done | bytes 6176 | tf_op jit(solution)/shard_map/ppermute | solution.py:25
  138.8 0.2 select_maximum_fusion.4
  139.3 0.2 fusion.18
  139.6 0.2 fusion.21
  140.1 3.9 %collective-permute-start.11 = (f32[3,1,512]{2,1,0:T(1,128)S(1)}, f32[3,1,512]{2,1,0:T(1,128)S(1)}, u32[]{:S(2)}, u32[]{:S(2)}) collective-permute-start(f32[3,1,512]{2,1,0:T(1,128)S(1)} %get-tuple-element.56), channel_id=1, source_target_pairs={{1,0},{2,1},{3,2},{4,3},{5,4},{6,5},{7,6},{9,8},{10,9},{11,10},{12... | collective-permute-start | bytes 18440 | tf_op jit(solution)/shard_map/ppermute | solution.py:26
  144.1 1.9 %collective-permute-start.10 = (f32[3,1,512]{2,1,0:T(1,128)S(1)}, f32[3,1,512]{2,1,0:T(1,128)S(1)}, u32[]{:S(2)}, u32[]{:S(2)}) collective-permute-start(f32[3,1,512]{2,1,0:T(1,128)S(1)} %get-tuple-element.55), channel_id=1, source_target_pairs={{0,1},{1,2},{2,3},{3,4},{4,5},{5,6},{6,7},{8,9},{9,10},{10,11},{11... | collective-permute-start | bytes 18440 | tf_op jit(solution)/shard_map/ppermute | solution.py:25
  146.0 4.5 %collective-permute-done.10 = f32[3,1,512]{2,1,0:T(1,128)S(1)} collective-permute-done((f32[3,1,512]{2,1,0:T(1,128)S(1)}, f32[3,1,512]{2,1,0:T(1,128)S(1)}, u32[]{:S(2)}, u32[]{:S(2)}) %collective-permute-start.10) | collective-permute-done | bytes 6176 | tf_op jit(solution)/shard_map/ppermute | solution.py:25
  151.0 0.2 fusion.13
  151.3 0.2 fusion.16
  151.8 0.7 maximum_bitcast_fusion
  (54 shorter events, 3.3 us)
Async XLA Ops:
  7.2 90.0 %all-gather.2.cloned.1.call-start = ((), (), s32[]{:S(2)}) async-start(), calls=%async_computation.1 | async-start | bytes 11796480 | tf_op jit(solution)/shard_map/all_gather | solution.py:112
  7.9 3.0 %collective-permute-start = (f32[3,128]{1,0:T(4,128)S(1)}, f32[3,128]{1,0:T(4,128)S(1)}, u32[]{:S(2)}, u32[]{:S(2)}) collective-permute-start(f32[3,128]{1,0:T(4,128)S(1)} %get-tuple-element.21), channel_id=1, source_target_pairs={{0,8},{8,16},{16,24},{1,9},{9,17},{17,25},{2,10},{10,18},{18,26},{... | collective-permute-start | bytes 4616 | tf_op jit(solution)/shard_map/ppermute | solution.py:25
  9.7 4.3 %collective-permute-start.1 = (f32[3,128]{1,0:T(4,128)S(1)}, f32[3,128]{1,0:T(4,128)S(1)}, u32[]{:S(2)}, u32[]{:S(2)}) collective-permute-start(f32[3,128]{1,0:T(4,128)S(1)} %get-tuple-element.20), channel_id=1, source_target_pairs={{8,0},{16,8},{24,16},{9,1},{17,9},{25,17},{10,2},{18,10},{26,18},{... | collective-permute-start | bytes 4616 | tf_op jit(solution)/shard_map/ppermute | solution.py:26
  16.7 6.1 %collective-permute-start.3 = (f32[1158,3]{0,1:T(4,128)S(1)}, f32[1158,3]{0,1:T(4,128)S(1)}, u32[]{:S(2)}, u32[]{:S(2)}) collective-permute-start(f32[1158,3]{0,1:T(4,128)S(1)} %copy.9), channel_id=1, source_target_pairs={{1,0},{2,1},{3,2},{4,3},{5,4},{6,5},{7,6},{9,8},{10,9},{11,10},{12... | collective-permute-start | bytes 41696 | tf_op jit(solution)/shard_map/ppermute | solution.py:26
  20.2 6.6 %collective-permute-start.2 = (f32[1158,3]{0,1:T(4,128)S(1)}, f32[1158,3]{0,1:T(4,128)S(1)}, u32[]{:S(2)}, u32[]{:S(2)}) collective-permute-start(f32[1158,3]{0,1:T(4,128)S(1)} %copy.8), channel_id=1, source_target_pairs={{0,1},{1,2},{2,3},{3,4},{4,5},{5,6},{6,7},{8,9},{9,10},{10,11},{11... | collective-permute-start | bytes 41696 | tf_op jit(solution)/shard_map/ppermute | solution.py:25
  31.9 0.8 copy-start
  31.9 0.9 copy-start.1
  32.8 7.2 %collective-permute-start.5 = (f32[3,1,512]{2,1,0:T(1,128)S(1)}, f32[3,1,512]{2,1,0:T(1,128)S(1)}, u32[]{:S(2)}, u32[]{:S(2)}) collective-permute-start(f32[3,1,512]{2,1,0:T(1,128)S(1)} %get-tuple-element.65), channel_id=1, source_target_pairs={{1,0},{2,1},{3,2},{4,3},{5,4},{6,5},{7,6},{9,8},{10,9},{11,10},{12... | collective-permute-start | bytes 18440 | tf_op jit(solution)/shard_map/ppermute | solution.py:26
  34.7 6.4 %collective-permute-start.4 = (f32[3,1,512]{2,1,0:T(1,128)S(1)}, f32[3,1,512]{2,1,0:T(1,128)S(1)}, u32[]{:S(2)}, u32[]{:S(2)}) collective-permute-start(f32[3,1,512]{2,1,0:T(1,128)S(1)} %get-tuple-element.64), channel_id=1, source_target_pairs={{0,1},{1,2},{2,3},{3,4},{4,5},{5,6},{6,7},{8,9},{9,10},{10,11},{11... | collective-permute-start | bytes 18440 | tf_op jit(solution)/shard_map/ppermute | solution.py:25
  99.1 18.2 %all-to-all-start = ((f32[4,8,32,128]{3,2,0,1:T(8,128)}), f32[4,8,32,128]{3,2,0,1:T(8,128)S(1)}, u32[]{:S(2)}, u32[]{:S(2)}) async-start(f32[4,8,32,128]{3,2,0,1:T(8,128)} %copy.12), calls=%async_computation | async-start | bytes 1048576 | tf_op jit(solution)/shard_map/all_to_all | solution.py:115
  117.9 5.9 %collective-permute-start.7 = (f32[3,1,512]{2,1,0:T(1,128)S(1)}, f32[3,1,512]{2,1,0:T(1,128)S(1)}, u32[]{:S(2)}, u32[]{:S(2)}) collective-permute-start(f32[3,1,512]{2,1,0:T(1,128)S(1)} %get-tuple-element.62), channel_id=1, source_target_pairs={{1,0},{2,1},{3,2},{4,3},{5,4},{6,5},{7,6},{9,8},{10,9},{11,10},{12... | collective-permute-start | bytes 18440 | tf_op jit(solution)/shard_map/ppermute | solution.py:26
  120.8 6.4 %collective-permute-start.6 = (f32[3,1,512]{2,1,0:T(1,128)S(1)}, f32[3,1,512]{2,1,0:T(1,128)S(1)}, u32[]{:S(2)}, u32[]{:S(2)}) collective-permute-start(f32[3,1,512]{2,1,0:T(1,128)S(1)} %get-tuple-element.61), channel_id=1, source_target_pairs={{0,1},{1,2},{2,3},{3,4},{4,5},{5,6},{6,7},{8,9},{9,10},{10,11},{11... | collective-permute-start | bytes 18440 | tf_op jit(solution)/shard_map/ppermute | solution.py:25
  128.6 5.9 %collective-permute-start.9 = (f32[3,1,512]{2,1,0:T(1,128)S(1)}, f32[3,1,512]{2,1,0:T(1,128)S(1)}, u32[]{:S(2)}, u32[]{:S(2)}) collective-permute-start(f32[3,1,512]{2,1,0:T(1,128)S(1)} %get-tuple-element.59), channel_id=1, source_target_pairs={{1,0},{2,1},{3,2},{4,3},{5,4},{6,5},{7,6},{9,8},{10,9},{11,10},{12... | collective-permute-start | bytes 18440 | tf_op jit(solution)/shard_map/ppermute | solution.py:26
  132.3 6.4 %collective-permute-start.8 = (f32[3,1,512]{2,1,0:T(1,128)S(1)}, f32[3,1,512]{2,1,0:T(1,128)S(1)}, u32[]{:S(2)}, u32[]{:S(2)}) collective-permute-start(f32[3,1,512]{2,1,0:T(1,128)S(1)} %get-tuple-element.58), channel_id=1, source_target_pairs={{0,1},{1,2},{2,3},{3,4},{4,5},{5,6},{6,7},{8,9},{9,10},{10,11},{11... | collective-permute-start | bytes 18440 | tf_op jit(solution)/shard_map/ppermute | solution.py:25
  140.1 5.9 %collective-permute-start.11 = (f32[3,1,512]{2,1,0:T(1,128)S(1)}, f32[3,1,512]{2,1,0:T(1,128)S(1)}, u32[]{:S(2)}, u32[]{:S(2)}) collective-permute-start(f32[3,1,512]{2,1,0:T(1,128)S(1)} %get-tuple-element.56), channel_id=1, source_target_pairs={{1,0},{2,1},{3,2},{4,3},{5,4},{6,5},{7,6},{9,8},{10,9},{11,10},{12... | collective-permute-start | bytes 18440 | tf_op jit(solution)/shard_map/ppermute | solution.py:26
  144.1 6.4 %collective-permute-start.10 = (f32[3,1,512]{2,1,0:T(1,128)S(1)}, f32[3,1,512]{2,1,0:T(1,128)S(1)}, u32[]{:S(2)}, u32[]{:S(2)}) collective-permute-start(f32[3,1,512]{2,1,0:T(1,128)S(1)} %get-tuple-element.55), channel_id=1, source_target_pairs={{0,1},{1,2},{2,3},{3,4},{4,5},{5,6},{6,7},{8,9},{9,10},{10,11},{11... | collective-permute-start | bytes 18440 | tf_op jit(solution)/shard_map/ppermute | solution.py:25
Sparse Core Ops, SparseCore 0:
  32.0 65.1 all-gather.1
where the time goes:
time: 160 us; the launch traced here: 159 us
  waiting for transfers between devices  87.3 us (55%)
  starting transfers between devices  38.3 us (24%)
  between operations  15.9 us (10%)
  other arithmetic  10.6 us (7%)
  local copies, waits for them, and re-layouts  7.37 us (5%)
    all_gather x1, waiting for transfers between devices, shards(): column_strip = lax.all_gather(ground_geometry, 'grp', axis=1, tiled=True)  55.6 us
    ppermute x6, waiting for transfers between devices, padded(): before = lax.ppermute(last, axis, up)  17.1 us
    ppermute x6, starting transfers between devices, padded(): after = lax.ppermute(leading, axis, down)  17.1 us
    ppermute x6, starting transfers between devices, padded(): before = lax.ppermute(last, axis, up)  15.2 us
    all_to_all x1, waiting for transfers between devices, shards(): lax.all_to_all(blocks, 'tile', split_axis=1, concat_axis=3, tiled=True)  11.5 us
    all_to_all x1, starting transfers between devices, shards(): lax.all_to_all(blocks, 'tile', split_axis=1, concat_axis=3, tiled=True)  6.03 us
  transfers between devices with their start and end apart: 14, of which 8 were waited for; matrix products, arithmetic and copies ran while one was open for 1% of the time, Pallas kernels for 0%

commit v1 on v0

--- a/solution.py
+++ b/solution.py
@@ -13,6 +13,35 @@
 depth_floor = 0.1
 speed_floor = 0.5
 binomial = (0.0625, 0.25, 0.375, 0.25, 0.0625)
+
+
+def _measure_pages(target, on_dim, here_x):
+    val = target.shape
+    e_next = target.reshape(*val[:on_dim], here_x, val[on_dim] // here_x, *val[on_dim + 1 :])
+    return jnp.moveaxis(e_next, on_dim, 0)
+
+
+def form_leaves_for(sheet, ndim_at):
+    sheet = jnp.moveaxis(sheet, 0, ndim_at)
+    piece_out = sheet.shape
+    return sheet.reshape(
+        *piece_out[:ndim_at], piece_out[ndim_at] * piece_out[ndim_at + 1], *piece_out[ndim_at + 2 :]
+    )
+
+
+def step_on_arrays(original, comm_axis, s0, work_x):
+    seen_now = jax.lax.axis_size(comm_axis)
+    tile_out = jax.lax.axis_index(comm_axis)
+    tmp, carry_in = (seen_now, tile_out)
+    finding = _measure_pages(original, s0, tmp)
+    bank = [finding[carry_in]]
+    for b in range(1, tmp):
+        extra = finding[carry_in ^ b]
+        a_next = jax.lax.ppermute(extra, comm_axis, [(ix, ix ^ b) for ix in range(tmp)])
+        bank.append(a_next)
+    ready = jnp.stack(bank)
+    finding = ready[carry_in ^ jnp.arange(tmp)]
+    return form_leaves_for(finding, work_x)
 
 
 def padded(shard, sides, width):
@@ -112,7 +141,7 @@
     column_strip = lax.all_gather(ground_geometry, "grp", axis=1, tiled=True)
     row_band = lax.dynamic_slice_in_dim(column_strip, first_row, window_height, 1)
     blocks = row_band.reshape(4, tile_count, piece_rows, block_lateral_number)
-    rows_wide = lax.all_to_all(blocks, "tile", split_axis=1, concat_axis=3, tiled=True)
+    rows_wide = step_on_arrays(blocks, "tile", 1, 3)
     rows_wide = rows_wide.reshape(4, piece_rows, tile_count * block_lateral_number)
     under_window = lax.dynamic_slice_in_dim(rows_wide, first_col, window_width, 2)
     release_depth = (

time: 160 us -> 157 us (0.981)
  waiting for transfers between devices: 87.3 us -> 80.2 us
  starting transfers between devices: 38.3 us -> 41.8 us
    all_to_all x1 -> x0, waiting for transfers between devices: 11.5 us -> none  [shards(): lax.all_to_all(blocks, 'tile', split_axis=1, concat_axis=3, tiled=True)]
    ppermute x0 -> x7, starting transfers between devices: none -> 9.53 us  [step_on_arrays(): jax.lax.ppermute(extra, comm_axis, [(ix, ix ^ b) for ix in range(tmp)])]
    ppermute x0 -> x7, waiting for transfers between devices: none -> 9 us  [step_on_arrays(): jax.lax.ppermute(extra, comm_axis, [(ix, ix ^ b) for ix in range(tmp)])]
    all_to_all x1 -> x0, starting transfers between devices: 6.03 us -> none  [shards(): lax.all_to_all(blocks, 'tile', split_axis=1, concat_axis=3, tiled=True)]
    ppermute x6, waiting for transfers between devices: 17.1 us -> 13.2 us  [padded(): before = lax.ppermute(last, axis, up)]
    ppermute x6, starting transfers between devices: 17.1 us -> 13.2 us  [padded(): after = lax.ppermute(leading, axis, down)]
    ppermute x6, starting transfers between devices: 15.2 us -> 19 us  [padded(): before = lax.ppermute(last, axis, up)]
  transfers between devices with their start and end apart: 14 -> 20, of which waited for: 8 -> 10; matrix products, arithmetic and copies ran while one was open for 1% -> 1% of each run, Pallas kernels for 0% -> 0%
where the time goes in v1:
time: 157 us; the launch traced here: 156 us
  waiting for transfers between devices  80.2 us (51%)
  starting transfers between devices  41.8 us (27%)
  between operations  16 us (10%)
  other arithmetic  10.6 us (7%)
  local copies, waits for them, and re-layouts  7.21 us (5%)
    all_gather x1, waiting for transfers between devices, shards(): column_strip = lax.all_gather(ground_geometry, 'grp', axis=1, tiled=True)  54.9 us
    ppermute x6, starting transfers between devices, padded(): before = lax.ppermute(last, axis, up)  19 us
    ppermute x6, starting transfers between devices, padded(): after = lax.ppermute(leading, axis, down)  13.2 us
    ppermute x6, waiting for transfers between devices, padded(): before = lax.ppermute(last, axis, up)  13.2 us
    ppermute x7, starting transfers between devices, step_on_arrays(): jax.lax.ppermute(extra, comm_axis, [(ix, ix ^ b) for ix in range(tmp)])  9.53 us
    ppermute x7, waiting for transfers between devices, step_on_arrays(): jax.lax.ppermute(extra, comm_axis, [(ix, ix ^ b) for ix in range(tmp)])  9 us
  transfers between devices with their start and end apart: 20, of which 10 were waited for; matrix products, arithmetic and copies ran while one was open for 1% of the time, Pallas kernels for 0%

profile of v1, /device:TPU:16, one launch (start us, length us, event | category | flops | bytes accessed | tf_op | source)
XLA Modules:
  0.0 155.8 jit_solution(16617698468363125629)
XLA Ops:
  7.2 0.7 fusion.59
  7.9 1.7 %collective-permute-start = (f32[3,128]{1,0:T(4,128)S(1)}, f32[3,128]{1,0:T(4,128)S(1)}, u32[]{:S(2)}, u32[]{:S(2)}) collective-permute-start(f32[3,128]{1,0:T(4,128)S(1)} %get-tuple-element.21), channel_id=1, source_target_pairs={{0,8},{8,16},{16,24},{1,9},{9,17},{17,25},{2,10},{10,18},{18,26},{... | collective-permute-start | bytes 4616 | tf_op jit(solution)/shard_map/ppermute | solution.py:54
  9.7 1.3 collective-permute-start.1
  11.0 3.0 %collective-permute-done.1 = f32[3,128]{1,0:T(4,128)S(1)} collective-permute-done((f32[3,128]{1,0:T(4,128)S(1)}, f32[3,128]{1,0:T(4,128)S(1)}, u32[]{:S(2)}, u32[]{:S(2)}) %collective-permute-start.1) | collective-permute-done | bytes 1568 | tf_op jit(solution)/shard_map/ppermute | solution.py:55
  14.0 2.3 %concatenate.42 = f32[1158,128]{1,0:T(8,128)S(1)} concatenate(f32[3,128]{1,0:T(4,128)S(1)} %collective-permute-done, f32[1152,128]{1,0:T(8,128)} %param.5, f32[3,128]{1,0:T(4,128)S(1)} %collective-permute-done.1), dimensions={0} | concatenate | bytes 1185792 | tf_op jit(solution)/shard_map/concatenate | solution.py:56
  16.3 0.2 fusion.58
  16.5 0.2 copy.9
  16.7 3.3 %collective-permute-start.3 = (f32[1158,3]{0,1:T(4,128)S(1)}, f32[1158,3]{0,1:T(4,128)S(1)}, u32[]{:S(2)}, u32[]{:S(2)}) collective-permute-start(f32[1158,3]{0,1:T(4,128)S(1)} %copy.9), channel_id=1, source_target_pairs={{1,0},{2,1},{3,2},{4,3},{5,4},{6,5},{7,6},{9,8},{10,9},{11,10},{12... | collective-permute-start | bytes 41696 | tf_op jit(solution)/shard_map/ppermute | solution.py:55
  20.0 0.2 copy.8
  20.2 2.5 %collective-permute-start.2 = (f32[1158,3]{0,1:T(4,128)S(1)}, f32[1158,3]{0,1:T(4,128)S(1)}, u32[]{:S(2)}, u32[]{:S(2)}) collective-permute-start(f32[1158,3]{0,1:T(4,128)S(1)} %copy.8), channel_id=1, source_target_pairs={{0,1},{1,2},{2,3},{3,4},{4,5},{5,6},{6,7},{8,9},{9,10},{10,11},{11... | collective-permute-start | bytes 41696 | tf_op jit(solution)/shard_map/ppermute | solution.py:54
  22.8 0.2 copy.11
  23.1 3.8 %collective-permute-done.2 = f32[1158,3]{0,1:T(4,128)S(1)} collective-permute-done((f32[1158,3]{0,1:T(4,128)S(1)}, f32[1158,3]{0,1:T(4,128)S(1)}, u32[]{:S(2)}, u32[]{:S(2)}) %collective-permute-start.2) | collective-permute-done | bytes 13928 | tf_op jit(solution)/shard_map/ppermute | solution.py:54
  26.8 0.2 copy.10
  27.1 0.5 pad_maximum_fusion.1
  27.6 0.7 fusion.4
  28.3 1.3 fusion
  29.6 0.7 multiply_bitcast_fusion.1
  30.3 1.6 %pad_maximum_fusion = f32[4,1152,128]{2,1,0:T(8,128)} fusion(f32[1,1152,128]{2,1,0:T(8,128)S(1)} %get-tuple-element.16, f32[1,1152,128]{2,1,0:T(8,128)S(1)} %get-tuple-element.15, f32[1,1152,128]{2,1,0:T(8,128)S(1)} %get-tuple-element.17, f32[1,1152,128]{2,1,0:T(8,128)S(1)} %get-tuple-element.14), kind=kLoop, calls=%fused_computation.1 | loop fusion | flops 1769472 | bytes 4718592 | tf_op jit(solution)/shard_map/stack | solution.py:82
  31.9 0.8 copy-done
  32.8 1.9 %collective-permute-start.5 = (f32[3,1,512]{2,1,0:T(1,128)S(1)}, f32[3,1,512]{2,1,0:T(1,128)S(1)}, u32[]{:S(2)}, u32[]{:S(2)}) collective-permute-start(f32[3,1,512]{2,1,0:T(1,128)S(1)} %get-tuple-element.72), channel_id=1, source_target_pairs={{1,0},{2,1},{3,2},{4,3},{5,4},{6,5},{7,6},{9,8},{10,9},{11,10},{12... | collective-permute-start | bytes 18440 | tf_op jit(solution)/shard_map/ppermute | solution.py:55
  34.7 3.9 %collective-permute-start.4 = (f32[3,1,512]{2,1,0:T(1,128)S(1)}, f32[3,1,512]{2,1,0:T(1,128)S(1)}, u32[]{:S(2)}, u32[]{:S(2)}) collective-permute-start(f32[3,1,512]{2,1,0:T(1,128)S(1)} %get-tuple-element.71), channel_id=1, source_target_pairs={{0,1},{1,2},{2,3},{3,4},{4,5},{5,6},{6,7},{8,9},{9,10},{10,11},{11... | collective-permute-start | bytes 18440 | tf_op jit(solution)/shard_map/ppermute | solution.py:54
  40.1 1.0 collective-permute-done.4
  42.2 54.9 %all-gather.2.cloned.1.call-done = f32[4,4608,128]{2,1,0:T(8,128)} async-done(((f32[4,1152,128]{2,1,0:T(8,128)}), f32[4,4608,128]{2,1,0:T(8,128)}) %all-gather.2.cloned.1.call-update) | async-done | bytes 9437200 | tf_op jit(solution)/shard_map/all_gather | solution.py:141
  97.2 1.1 constant_dynamic-slice_fusion
  98.3 1.5 collective-permute-start.6
  99.9 1.5 collective-permute-start.7
  101.4 0.5 collective-permute-start.8
  101.9 0.5 collective-permute-start.9
  102.4 3.3 %collective-permute-start.10 = (f32[4,1,32,128]{3,2,0,1:T(8,128)S(1)}, f32[4,1,32,128]{3,2,0,1:T(8,128)S(1)}, u32[]{:S(2)}, u32[]{:S(2)}) collective-permute-start(f32[4,1,32,128]{3,2,0,1:T(8,128)S(1)} %get-tuple-element.24), channel_id=1, source_target_pairs={{0,5},{1,4},{2,7},{3,6},{4,1},{5,0},{6,3},{7,2},{8,13},{9,12},{10,... | collective-permute-start | bytes 196616 | tf_op jit(solution)/shard_map/ppermute | solution.py:40
  105.7 0.6 collective-permute-start.11
  106.4 1.5 collective-permute-start.12
  108.0 2.9 %collective-permute-done.10 = f32[4,1,32,128]{3,2,0,1:T(8,128)S(1)} collective-permute-done((f32[4,1,32,128]{3,2,0,1:T(8,128)S(1)}, f32[4,1,32,128]{3,2,0,1:T(8,128)S(1)}, u32[]{:S(2)}, u32[]{:S(2)}) %collective-permute-start.10) | collective-permute-done | bytes 65568 | tf_op jit(solution)/shard_map/ppermute | solution.py:40
  110.9 4.4 %collective-permute-done.11 = f32[4,1,32,128]{3,2,0,1:T(8,128)S(1)} collective-permute-done((f32[4,1,32,128]{3,2,0,1:T(8,128)S(1)}, f32[4,1,32,128]{3,2,0,1:T(8,128)S(1)}, u32[]{:S(2)}, u32[]{:S(2)}) %collective-permute-start.11) | collective-permute-done | bytes 65568 | tf_op jit(solution)/shard_map/ppermute | solution.py:40
  115.2 1.7 %collective-permute-done.12 = f32[4,1,32,128]{3,2,0,1:T(8,128)S(1)} collective-permute-done((f32[4,1,32,128]{3,2,0,1:T(8,128)S(1)}, f32[4,1,32,128]{3,2,0,1:T(8,128)S(1)}, u32[]{:S(2)}, u32[]{:S(2)}) %collective-permute-start.12) | collective-permute-done | bytes 65568 | tf_op jit(solution)/shard_map/ppermute | solution.py:40
  117.0 0.6 gather_fusion
  117.5 0.3 copy.12
  118.2 2.5 %collective-permute-start.14 = (f32[3,1,512]{2,1,0:T(1,128)S(1)}, f32[3,1,512]{2,1,0:T(1,128)S(1)}, u32[]{:S(2)}, u32[]{:S(2)}) collective-permute-start(f32[3,1,512]{2,1,0:T(1,128)S(1)} %get-tuple-element.69), channel_id=1, source_target_pairs={{1,0},{2,1},{3,2},{4,3},{5,4},{6,5},{7,6},{9,8},{10,9},{11,10},{12... | collective-permute-start | bytes 18440 | tf_op jit(solution)/shard_map/ppermute | solution.py:55
  120.7 3.3 %collective-permute-start.13 = (f32[3,1,512]{2,1,0:T(1,128)S(1)}, f32[3,1,512]{2,1,0:T(1,128)S(1)}, u32[]{:S(2)}, u32[]{:S(2)}) collective-permute-start(f32[3,1,512]{2,1,0:T(1,128)S(1)} %get-tuple-element.68), channel_id=1, source_target_pairs={{0,1},{1,2},{2,3},{3,4},{4,5},{5,6},{6,7},{8,9},{9,10},{10,11},{11... | collective-permute-start | bytes 18440 | tf_op jit(solution)/shard_map/ppermute | solution.py:54
  124.1 3.1 %collective-permute-done.13 = f32[3,1,512]{2,1,0:T(1,128)S(1)} collective-permute-done((f32[3,1,512]{2,1,0:T(1,128)S(1)}, f32[3,1,512]{2,1,0:T(1,128)S(1)}, u32[]{:S(2)}, u32[]{:S(2)}) %collective-permute-start.13) | collective-permute-done | bytes 6176 | tf_op jit(solution)/shard_map/ppermute | solution.py:54
  128.5 2.2 %collective-permute-start.16 = (f32[3,1,512]{2,1,0:T(1,128)S(1)}, f32[3,1,512]{2,1,0:T(1,128)S(1)}, u32[]{:S(2)}, u32[]{:S(2)}) collective-permute-start(f32[3,1,512]{2,1,0:T(1,128)S(1)} %get-tuple-element.66), channel_id=1, source_target_pairs={{1,0},{2,1},{3,2},{4,3},{5,4},{6,5},{7,6},{9,8},{10,9},{11,10},{12... | collective-permute-start | bytes 18440 | tf_op jit(solution)/shard_map/ppermute | solution.py:55
  130.7 3.7 %collective-permute-start.15 = (f32[3,1,512]{2,1,0:T(1,128)S(1)}, f32[3,1,512]{2,1,0:T(1,128)S(1)}, u32[]{:S(2)}, u32[]{:S(2)}) collective-permute-start(f32[3,1,512]{2,1,0:T(1,128)S(1)} %get-tuple-element.65), channel_id=1, source_target_pairs={{0,1},{1,2},{2,3},{3,4},{4,5},{5,6},{6,7},{8,9},{9,10},{10,11},{11... | collective-permute-start | bytes 18440 | tf_op jit(solution)/shard_map/ppermute | solution.py:54
  134.4 2.7 %collective-permute-done.15 = f32[3,1,512]{2,1,0:T(1,128)S(1)} collective-permute-done((f32[3,1,512]{2,1,0:T(1,128)S(1)}, f32[3,1,512]{2,1,0:T(1,128)S(1)}, u32[]{:S(2)}, u32[]{:S(2)}) %collective-permute-start.15) | collective-permute-done | bytes 6176 | tf_op jit(solution)/shard_map/ppermute | solution.py:54
  137.9 0.2 fusion.21
  138.5 2.0 %collective-permute-start.18 = (f32[3,1,512]{2,1,0:T(1,128)S(1)}, f32[3,1,512]{2,1,0:T(1,128)S(1)}, u32[]{:S(2)}, u32[]{:S(2)}) collective-permute-start(f32[3,1,512]{2,1,0:T(1,128)S(1)} %get-tuple-element.63), channel_id=1, source_target_pairs={{1,0},{2,1},{3,2},{4,3},{5,4},{6,5},{7,6},{9,8},{10,9},{11,10},{12... | collective-permute-start | bytes 18440 | tf_op jit(solution)/shard_map/ppermute | solution.py:55
  140.5 3.8 %collective-permute-start.17 = (f32[3,1,512]{2,1,0:T(1,128)S(1)}, f32[3,1,512]{2,1,0:T(1,128)S(1)}, u32[]{:S(2)}, u32[]{:S(2)}) collective-permute-start(f32[3,1,512]{2,1,0:T(1,128)S(1)} %get-tuple-element.62), channel_id=1, source_target_pairs={{0,1},{1,2},{2,3},{3,4},{4,5},{5,6},{6,7},{8,9},{9,10},{10,11},{11... | collective-permute-start | bytes 18440 | tf_op jit(solution)/shard_map/ppermute | solution.py:54
  144.3 2.6 %collective-permute-done.17 = f32[3,1,512]{2,1,0:T(1,128)S(1)} collective-permute-done((f32[3,1,512]{2,1,0:T(1,128)S(1)}, f32[3,1,512]{2,1,0:T(1,128)S(1)}, u32[]{:S(2)}, u32[]{:S(2)}) %collective-permute-start.17) | collective-permute-done | bytes 6176 | tf_op jit(solution)/shard_map/ppermute | solution.py:54
  147.7 0.2 fusion.16
  148.2 0.7 maximum_bitcast_fusion
  (77 shorter events, 5.1 us)
Async XLA Ops:
  7.2 90.0 %all-gather.2.cloned.1.call-start = ((), (), s32[]{:S(2)}) async-start(), calls=%async_computation | async-start | bytes 11796480 | tf_op jit(solution)/shard_map/all_gather | solution.py:141
  7.9 3.0 %collective-permute-start = (f32[3,128]{1,0:T(4,128)S(1)}, f32[3,128]{1,0:T(4,128)S(1)}, u32[]{:S(2)}, u32[]{:S(2)}) collective-permute-start(f32[3,128]{1,0:T(4,128)S(1)} %get-tuple-element.21), channel_id=1, source_target_pairs={{0,8},{8,16},{16,24},{1,9},{9,17},{17,25},{2,10},{10,18},{18,26},{... | collective-permute-start | bytes 4616 | tf_op jit(solution)/shard_map/ppermute | solution.py:54
  9.7 4.3 %collective-permute-start.1 = (f32[3,128]{1,0:T(4,128)S(1)}, f32[3,128]{1,0:T(4,128)S(1)}, u32[]{:S(2)}, u32[]{:S(2)}) collective-permute-start(f32[3,128]{1,0:T(4,128)S(1)} %get-tuple-element.20), channel_id=1, source_target_pairs={{8,0},{16,8},{24,16},{9,1},{17,9},{25,17},{10,2},{18,10},{26,18},{... | collective-permute-start | bytes 4616 | tf_op jit(solution)/shard_map/ppermute | solution.py:55
  16.7 6.1 %collective-permute-start.3 = (f32[1158,3]{0,1:T(4,128)S(1)}, f32[1158,3]{0,1:T(4,128)S(1)}, u32[]{:S(2)}, u32[]{:S(2)}) collective-permute-start(f32[1158,3]{0,1:T(4,128)S(1)} %copy.9), channel_id=1, source_target_pairs={{1,0},{2,1},{3,2},{4,3},{5,4},{6,5},{7,6},{9,8},{10,9},{11,10},{12... | collective-permute-start | bytes 41696 | tf_op jit(solution)/shard_map/ppermute | solution.py:55
  20.2 6.6 %collective-permute-start.2 = (f32[1158,3]{0,1:T(4,128)S(1)}, f32[1158,3]{0,1:T(4,128)S(1)}, u32[]{:S(2)}, u32[]{:S(2)}) collective-permute-start(f32[1158,3]{0,1:T(4,128)S(1)} %copy.8), channel_id=1, source_target_pairs={{0,1},{1,2},{2,3},{3,4},{4,5},{5,6},{6,7},{8,9},{9,10},{10,11},{11... | collective-permute-start | bytes 41696 | tf_op jit(solution)/shard_map/ppermute | solution.py:54
  31.9 0.8 copy-start
  31.9 0.9 copy-start.1
  32.8 7.3 %collective-permute-start.5 = (f32[3,1,512]{2,1,0:T(1,128)S(1)}, f32[3,1,512]{2,1,0:T(1,128)S(1)}, u32[]{:S(2)}, u32[]{:S(2)}) collective-permute-start(f32[3,1,512]{2,1,0:T(1,128)S(1)} %get-tuple-element.72), channel_id=1, source_target_pairs={{1,0},{2,1},{3,2},{4,3},{5,4},{6,5},{7,6},{9,8},{10,9},{11,10},{12... | collective-permute-start | bytes 18440 | tf_op jit(solution)/shard_map/ppermute | solution.py:55
  34.7 6.4 %collective-permute-start.4 = (f32[3,1,512]{2,1,0:T(1,128)S(1)}, f32[3,1,512]{2,1,0:T(1,128)S(1)}, u32[]{:S(2)}, u32[]{:S(2)}) collective-permute-start(f32[3,1,512]{2,1,0:T(1,128)S(1)} %get-tuple-element.71), channel_id=1, source_target_pairs={{0,1},{1,2},{2,3},{3,4},{4,5},{5,6},{6,7},{8,9},{9,10},{10,11},{11... | collective-permute-start | bytes 18440 | tf_op jit(solution)/shard_map/ppermute | solution.py:54
  98.3 7.4 %collective-permute-start.6 = (f32[4,1,32,128]{3,2,0,1:T(8,128)S(1)}, f32[4,1,32,128]{3,2,0,1:T(8,128)S(1)}, u32[]{:S(2)}, u32[]{:S(2)}) collective-permute-start(f32[4,1,32,128]{3,2,0,1:T(8,128)S(1)} %get-tuple-element.28), channel_id=1, source_target_pairs={{0,1},{1,0},{2,3},{3,2},{4,5},{5,4},{6,7},{7,6},{8,9},{9,8},{10,11... | collective-permute-start | bytes 196616 | tf_op jit(solution)/shard_map/ppermute | solution.py:40
  99.9 6.5 %collective-permute-start.7 = (f32[4,1,32,128]{3,2,0,1:T(8,128)S(1)}, f32[4,1,32,128]{3,2,0,1:T(8,128)S(1)}, u32[]{:S(2)}, u32[]{:S(2)}) collective-permute-start(f32[4,1,32,128]{3,2,0,1:T(8,128)S(1)} %get-tuple-element.27), channel_id=1, source_target_pairs={{0,2},{1,3},{2,0},{3,1},{4,6},{5,7},{6,4},{7,5},{8,10},{9,11},{10,... | collective-permute-start | bytes 196616 | tf_op jit(solution)/shard_map/ppermute | solution.py:40
  101.4 6.5 %collective-permute-start.8 = (f32[4,1,32,128]{3,2,0,1:T(8,128)S(1)}, f32[4,1,32,128]{3,2,0,1:T(8,128)S(1)}, u32[]{:S(2)}, u32[]{:S(2)}) collective-permute-start(f32[4,1,32,128]{3,2,0,1:T(8,128)S(1)} %get-tuple-element.26), channel_id=1, source_target_pairs={{0,3},{1,2},{2,1},{3,0},{4,7},{5,6},{6,5},{7,4},{8,11},{9,10},{10,... | collective-permute-start | bytes 196616 | tf_op jit(solution)/shard_map/ppermute | solution.py:40
  101.9 6.0 %collective-permute-start.9 = (f32[4,1,32,128]{3,2,0,1:T(8,128)S(1)}, f32[4,1,32,128]{3,2,0,1:T(8,128)S(1)}, u32[]{:S(2)}, u32[]{:S(2)}) collective-permute-start(f32[4,1,32,128]{3,2,0,1:T(8,128)S(1)} %get-tuple-element.25), channel_id=1, source_target_pairs={{0,4},{1,5},{2,6},{3,7},{4,0},{5,1},{6,2},{7,3},{8,12},{9,13},{10,... | collective-permute-start | bytes 196616 | tf_op jit(solution)/shard_map/ppermute | solution.py:40
  102.4 8.4 %collective-permute-start.10 = (f32[4,1,32,128]{3,2,0,1:T(8,128)S(1)}, f32[4,1,32,128]{3,2,0,1:T(8,128)S(1)}, u32[]{:S(2)}, u32[]{:S(2)}) collective-permute-start(f32[4,1,32,128]{3,2,0,1:T(8,128)S(1)} %get-tuple-element.24), channel_id=1, source_target_pairs={{0,5},{1,4},{2,7},{3,6},{4,1},{5,0},{6,3},{7,2},{8,13},{9,12},{10,... | collective-permute-start | bytes 196616 | tf_op jit(solution)/shard_map/ppermute | solution.py:40
  105.7 9.5 %collective-permute-start.11 = (f32[4,1,32,128]{3,2,0,1:T(8,128)S(1)}, f32[4,1,32,128]{3,2,0,1:T(8,128)S(1)}, u32[]{:S(2)}, u32[]{:S(2)}) collective-permute-start(f32[4,1,32,128]{3,2,0,1:T(8,128)S(1)} %get-tuple-element.23), channel_id=1, source_target_pairs={{0,6},{1,7},{2,4},{3,5},{4,2},{5,3},{6,0},{7,1},{8,14},{9,15},{10,... | collective-permute-start | bytes 196616 | tf_op jit(solution)/shard_map/ppermute | solution.py:40
  106.4 10.6 %collective-permute-start.12 = (f32[4,1,32,128]{3,2,0,1:T(8,128)S(1)}, f32[4,1,32,128]{3,2,0,1:T(8,128)S(1)}, u32[]{:S(2)}, u32[]{:S(2)}) collective-permute-start(f32[4,1,32,128]{3,2,0,1:T(8,128)S(1)} %get-tuple-element.22), channel_id=1, source_target_pairs={{0,7},{1,6},{2,5},{3,4},{4,3},{5,2},{6,1},{7,0},{8,15},{9,14},{10,... | collective-permute-start | bytes 196616 | tf_op jit(solution)/shard_map/ppermute | solution.py:40
  118.2 5.9 %collective-permute-start.14 = (f32[3,1,512]{2,1,0:T(1,128)S(1)}, f32[3,1,512]{2,1,0:T(1,128)S(1)}, u32[]{:S(2)}, u32[]{:S(2)}) collective-permute-start(f32[3,1,512]{2,1,0:T(1,128)S(1)} %get-tuple-element.69), channel_id=1, source_target_pairs={{1,0},{2,1},{3,2},{4,3},{5,4},{6,5},{7,6},{9,8},{10,9},{11,10},{12... | collective-permute-start | bytes 18440 | tf_op jit(solution)/shard_map/ppermute | solution.py:55
  120.7 6.4 %collective-permute-start.13 = (f32[3,1,512]{2,1,0:T(1,128)S(1)}, f32[3,1,512]{2,1,0:T(1,128)S(1)}, u32[]{:S(2)}, u32[]{:S(2)}) collective-permute-start(f32[3,1,512]{2,1,0:T(1,128)S(1)} %get-tuple-element.68), channel_id=1, source_target_pairs={{0,1},{1,2},{2,3},{3,4},{4,5},{5,6},{6,7},{8,9},{9,10},{10,11},{11... | collective-permute-start | bytes 18440 | tf_op jit(solution)/shard_map/ppermute | solution.py:54
  128.5 5.9 %collective-permute-start.16 = (f32[3,1,512]{2,1,0:T(1,128)S(1)}, f32[3,1,512]{2,1,0:T(1,128)S(1)}, u32[]{:S(2)}, u32[]{:S(2)}) collective-permute-start(f32[3,1,512]{2,1,0:T(1,128)S(1)} %get-tuple-element.66), channel_id=1, source_target_pairs={{1,0},{2,1},{3,2},{4,3},{5,4},{6,5},{7,6},{9,8},{10,9},{11,10},{12... | collective-permute-start | bytes 18440 | tf_op jit(solution)/shard_map/ppermute | solution.py:55
  130.7 6.4 %collective-permute-start.15 = (f32[3,1,512]{2,1,0:T(1,128)S(1)}, f32[3,1,512]{2,1,0:T(1,128)S(1)}, u32[]{:S(2)}, u32[]{:S(2)}) collective-permute-start(f32[3,1,512]{2,1,0:T(1,128)S(1)} %get-tuple-element.65), channel_id=1, source_target_pairs={{0,1},{1,2},{2,3},{3,4},{4,5},{5,6},{6,7},{8,9},{9,10},{10,11},{11... | collective-permute-start | bytes 18440 | tf_op jit(solution)/shard_map/ppermute | solution.py:54
  138.5 5.9 %collective-permute-start.18 = (f32[3,1,512]{2,1,0:T(1,128)S(1)}, f32[3,1,512]{2,1,0:T(1,128)S(1)}, u32[]{:S(2)}, u32[]{:S(2)}) collective-permute-start(f32[3,1,512]{2,1,0:T(1,128)S(1)} %get-tuple-element.63), channel_id=1, source_target_pairs={{1,0},{2,1},{3,2},{4,3},{5,4},{6,5},{7,6},{9,8},{10,9},{11,10},{12... | collective-permute-start | bytes 18440 | tf_op jit(solution)/shard_map/ppermute | solution.py:55
  140.5 6.4 %collective-permute-start.17 = (f32[3,1,512]{2,1,0:T(1,128)S(1)}, f32[3,1,512]{2,1,0:T(1,128)S(1)}, u32[]{:S(2)}, u32[]{:S(2)}) collective-permute-start(f32[3,1,512]{2,1,0:T(1,128)S(1)} %get-tuple-element.62), channel_id=1, source_target_pairs={{0,1},{1,2},{2,3},{3,4},{4,5},{5,6},{6,7},{8,9},{9,10},{10,11},{11... | collective-permute-start | bytes 18440 | tf_op jit(solution)/shard_map/ppermute | solution.py:54
Sparse Core Ops, SparseCore 0:
  32.0 65.1 all-gather.1
